TPU v7x, 128 devices: a whole 4x4x4 slice. The times are simulated.
128 devices in a mesh: grp: 4 (over y), dev: 32 (over z, x, core).
Axes of the slice: x: 4, y: 4, z: 4, core: 2. Of those that a mesh axis runs over, the one named last changes fastest.
Arguments:
- points: float32 [64, 196608], P(None, 'dev'), may hold values from -6 to 6
- weights: float32 [196608, 128], P('dev'), may hold values from -4 to 4
- proj: float32 [256, 196608], P(None, 'dev'), may hold values from -0.078125 to 0.078125
- fetch_table: int32 [3, 32, 32, 2], P(None, 'dev'), may hold values from 0 to 11, as said below
- near_list: int32 [384, 16], P('dev'), may hold values from 0 to 63, as said below
- far_list: int32 [384, 8], P('dev'), may hold values from 0 to 31, as said below
- skel_idx: int32 [32, 256], P('dev'), may hold values from 0 to 6143, as said below
Outputs:
- potential: float32 [196608, 128], P('dev')
Inputs may be any that keep to these rules, and one draw needn't show every extreme that they name: Entries of fetch_table[r, d, e] are distinct local leaf numbers of column e. `near_list`: the 16 slots of one target leaf are distinct. `far_list`: the 8 nodes of one target leaf are distinct, and one of them is node (c + 1) mod 32 for the leaf's column c. `skel_idx`: the 256 skeleton points of one node are distinct.
All inputs are finite; a program needn't handle non-finite values.
Results may differ from a plain program's by a relative error of at most 0.0003.
Values sent between devices are 32-bit elements; how exact they have to be, the bound alone decides.
A program may use at most 192 MiB of HBM per device.

v0:
```python
import jax
import jax.numpy as jnp
from jax import lax
from jax.sharding import PartitionSpec as P


def kernel_sum(target, sources, values):
    high = lax.Precision.HIGHEST
    inner = jnp.einsum("dt,jds->tjs", target, sources, precision=high)
    target_norm = jnp.sum(target * target, axis=0)
    source_norm = jnp.sum(sources * sources, axis=1)
    distance = target_norm[:, None, None] + source_norm[None] - 2.0 * inner
    kernel = jnp.exp(-distance * (2.0 / target.shape[0]))
    return jnp.einsum("tjs,jsw->tw", kernel, values, precision=high)


def on_device(points, weights, proj, fetch_table, near_list, far_list, skel_idx):
    features, column_points = points.shape
    columns = weights.shape[1]
    devices = lax.axis_size("dev")
    groups = lax.axis_size("grp")
    targets = near_list.shape[0]
    leaf_size = column_points // targets
    row_leaves = targets // (groups - 1)
    capacity = fetch_table.shape[3]
    skeleton = skel_idx.shape[1]
    group_index = lax.axis_index("grp")
    near_row = jnp.minimum(group_index, groups - 2)
    far_side = group_index == groups - 1
    leaf_coords = points.reshape(features, targets, leaf_size)
    leaf_weights = weights.reshape(targets, leaf_size, columns)
    requests = lax.dynamic_index_in_dim(fetch_table[:, 0], near_row, 0, keepdims=False)
    asked = lax.all_to_all(requests, "dev", split_axis=0, concat_axis=0, tiled=True)
    coords = jnp.moveaxis(jnp.take(leaf_coords, asked, axis=1), 0, 2)
    values = jnp.take(leaf_weights, asked, axis=0)
    fetched_coords = lax.all_to_all(coords, "dev", split_axis=0, concat_axis=0, tiled=True)
    fetched_values = lax.all_to_all(values, "dev", split_axis=0, concat_axis=0, tiled=True)
    flat_coords = fetched_coords.reshape(devices * capacity, features, leaf_size)
    flat_values = fetched_values.reshape(devices * capacity, leaf_size, columns)
    local_skeleton = jnp.take(points, skel_idx[0], axis=1)
    share_len = column_points // groups
    share_start = group_index * share_len
    share_proj = lax.dynamic_slice_in_dim(proj, share_start, share_len, 1)
    share_weights = lax.dynamic_slice_in_dim(weights, share_start, share_len, 0)
    partial_value = jnp.dot(
        share_proj,
        share_weights,
        preferred_element_type=jnp.float32,
        precision=lax.Precision.HIGHEST,
    )
    node_index = lax.axis_index("dev")
    owner_mask = jnp.where(far_side, 1.0, 0.0).astype(jnp.float32)
    table_coords = jnp.zeros((devices, features, skeleton), jnp.float32)
    table_coords = lax.dynamic_update_index_in_dim(
        table_coords, local_skeleton * owner_mask, node_index, 0
    )
    table_weights = jnp.zeros((devices, skeleton, columns), jnp.float32)
    table_weights = lax.dynamic_update_index_in_dim(table_weights, partial_value, node_index, 0)
    skel_coords, skel_weights = lax.psum((table_coords, table_weights), ("grp", "dev"))

    def near_work():
        slots = lax.dynamic_slice_in_dim(near_list, near_row * row_leaves, row_leaves, 0)
        leaf_numbers = near_row * row_leaves + jnp.arange(row_leaves, dtype=jnp.int32)

        def near_leaf(items):
            leaf_number, leaf_slots = items
            target = jnp.take(leaf_coords, leaf_number, axis=1)
            return kernel_sum(
                target,
                jnp.take(flat_coords, leaf_slots, axis=0),
                jnp.take(flat_values, leaf_slots, axis=0),
            )

        block = lax.map(near_leaf, (leaf_numbers, slots))
        empty = jnp.zeros((targets, leaf_size, columns), jnp.float32)
        return lax.dynamic_update_slice_in_dim(empty, block, near_row * row_leaves, 0)

    def far_work():

        def far_leaf(items):
            leaf_number, node_ids = items
            target = jnp.take(leaf_coords, leaf_number, axis=1)
            return kernel_sum(
                target,
                jnp.take(skel_coords, node_ids, axis=0),
                jnp.take(skel_weights, node_ids, axis=0),
            )

        return lax.map(far_leaf, (jnp.arange(targets, dtype=jnp.int32), far_list))

    contribution = lax.cond(far_side, far_work, near_work)
    total = lax.psum(contribution, "grp")
    return total.reshape(column_points, columns)


def solution(mesh):
    placed = (
        P(None, "dev"),
        P("dev", None),
        P(None, "dev"),
        P(None, "dev", None, None),
        P("dev", None),
        P("dev", None),
        P("dev", None),
    )
    return jax.shard_map(
        on_device, mesh=mesh, in_specs=placed, out_specs=P("dev", None), check_vma=False
    )
```

profile of v0, /device:TPU:1, one launch (start us, length us, event | category | flops | bytes accessed | tf_op | source)
XLA Modules:
  0.0 820.4 jit_solution(13350892789192930071)
XLA Ops:
  6.5 0.8 fusion.82
  7.4 0.7 copy.36
  8.1 9.4 %all-to-all-start = ((s32[32,1,2]{2,1,0:T(1,128)}), s32[32,1,2]{2,1,0:T(1,128)S(1)}, u32[]{:S(2)}, u32[]{:S(2)}) async-start(s32[32,1,2]{2,1,0:T(1,128)} %copy.36), calls=%async_computation | async-start | bytes 32768 | tf_op jit(solution)/shard_map/all_to_all | solution.py:33
  17.5 2.7 copy.64
  20.2 4.2 all-to-all-done
  24.4 0.1 copy.37
  24.5 0.1 copy.40
  24.6 0.1 reshape.285
  24.7 0.1 copy.38
  24.8 5.7 gather_fusion.4
  30.6 8.5 %broadcast_select_fusion.1 = f32[32,2,64,512]{3,2,1,0:T(8,128)} fusion(f32[32,2,64,512]{3,2,1,0:T(8,128)} %bitcast.103, pred[32,2]{1,0:T(8,128)(4,1)S(1)} %copy.38), kind=kLoop, calls=%fused_computation.87 | loop fusion | flops 2097152 | bytes 16777280 | tf_op jit(solution)/shard_map/jit(_take)/select_n | solution.py:34
  39.1 5.2 all-to-all-start.1
  44.3 7.4 gather_fusion.5
  51.6 11.6 %broadcast_select_fusion = f32[32,2,512,128]{3,2,1,0:T(8,128)} fusion(f32[32,2,512,128]{3,2,1,0:T(8,128)} %bitcast.101, pred[32,2]{1,0:T(8,128)(4,1)S(1)} %copy.38), kind=kLoop, calls=%fused_computation.86 | loop fusion | flops 4194304 | bytes 33554496 | tf_op jit(solution)/shard_map/jit(_take)/select_n | solution.py:35
  63.2 80.8 %all-to-all-done.1 = f32[32,2,64,512]{3,2,1,0:T(8,128)} async-done(((f32[32,2,64,512]{3,2,1,0:T(8,128)}), f32[32,2,64,512]{3,2,1,0:T(8,128)}, u32[]{:S(2)}, u32[]{:S(2)}) %all-to-all-start.1) | async-done | bytes 8388640 | tf_op jit(solution)/shard_map/all_to_all | solution.py:36
  144.0 11.3 %all-to-all-start.2 = ((f32[32,2,512,128]{3,2,1,0:T(8,128)}), f32[32,2,512,128]{3,2,1,0:T(8,128)}, u32[]{:S(2)}, u32[]{:S(2)}) async-start(f32[32,2,512,128]{3,2,1,0:T(8,128)} %broadcast_select_fusion), calls=%async_computation.2 | async-start | bytes 33554432 | tf_op jit(solution)/shard_map/all_to_all | solution.py:37
  155.3 0.0 all-reduce.6.cloned.1.call-start
  155.4 3.3 copy.43
  158.6 2.6 gather_fusion.6
  161.3 0.1 copy.44
  161.3 2.4 broadcast_in_dim.110
  163.8 3.5 fusion.75
  167.2 1.6 broadcast_in_dim.107
  168.8 0.6 fusion.80
  169.4 0.0 all-reduce.6.cloned.1.call-update
  169.5 0.0 all-reduce.4.cloned.1.call-start
  169.5 1.9 reshape.193
  171.4 310.3 %all-reduce.6.cloned.1.call-done = (f32[32,64,256]{2,1,0:T(8,128)}, f32[32,256,128]{2,1,0:T(8,128)}) async-done(((f32[32,64,256]{2,1,0:T(8,128)}, f32[32,256,128]{2,1,0:T(8,128)}), (f32[32,64,256]{2,1,0:T(8,128)}, f32[32,256,128]{2,1,0:T(8,128)})) %all-reduce.6.cloned.1.call-update) | async-done | bytes 6291472 | tf_op jit(solution)/shard_map/psum | solution.py:59
  481.8 223.2 %conditional.1 = (f32[12,512,128]{2,1,0:T(8,128)}) conditional(s32[]{:T(128)} %convert_element_type.3, (s32[]{:T(128)}, s32[12,16]{1,0:T(8,128)}, f32[32,2,64,512]{3,2,1,0:T(8,128)}, f32[32,2,512,128]{3,2,1,0:T(8,128)}, f32[64,12,512]{2,1,0:T(8,128)}) %tuple.20, (f32[64,12,512]{2,1,0:T(8,128)}, s32[12,8]{0,1:T(8,128)S(1)}, f32[32,64,256]{2,1,0:T(8,128)}, ...), branch_computations={%region_2.0_spmd, %region_7.13_spmd} | conditional | flops 9687917568 | bytes 60630836 | solution.py:91
  481.8 0.7 constant_dynamic-slice_fusion.2
  482.4 218.3 %while.19 = (s32[]{:T(128)}, f32[4,512,128]{2,1,0:T(8,128)}, s32[4]{0:T(128)S(1)}, f32[64,12,512]{2,1,0:T(8,128)}, s32[4,16]{1,0:T(4,128)S(1)}, /*index=5*/f32[6...) while((s32[]{:T(128)}, f32[4,512,128]{2,1,0:T(8,128)}, ...), condition=%wide.region_6.7_spmd, body=%wide.region_3.6_spmd.sunk | while | flops 9687917568 | bytes 55387260 | solution.py:74
  482.5 0.6 dynamic_slice.65
  484.9 1.3 constant_dynamic-slice_fusion.9
  486.3 4.1 gather_fusion.3
  490.4 16.2 %fusion.112 = f32[512,16,512]{2,0,1:T(8,128)} fusion(f32[16,64,512]{2,1,0:T(8,128)S(1)} %gather_fusion.3, pred[16]{0:T(512)(128)(4,1)S(1)} %compare_and_fusion.7, f32[64,1,512]{2,1,0:T(1,128)S(1)} %constant_dynamic-slice_fusion.9, pred[]{:T(512)S(6)} %and.57), kind=kOutput, calls=%fused_computation.22.clone.1 | convolution fusion | flops 3221782528 | bytes 19005456 | tf_op jit(solution)/shard_map/cond/branch_0_fun/while/body/eval_jaxpr/dt,jds->tjs/dot_general | solution.py:9
  506.6 0.4 multiply_reduce_fusion.5
  507.0 8.5 %gather_fusion.2 = f32[16,512,128]{2,1,0:T(8,128)} fusion(f32[64,512,128]{2,1,0:T(8,128)} %get-tuple-element.330, s32[1024]{0:T(1024)S(1)} %pad_clamp_fusion.7), kind=kCustom, calls=%fused_computation.1.clone.1 | custom fusion | bytes 8388672 | tf_op jit(solution)/shard_map/cond/branch_0_fun/while/body/eval_jaxpr/jit(_take)/gather | solution.py:71
  515.5 21.5 %fusion.114 = f32[4,512,128]{2,1,0:T(8,128)} fusion(f32[4,512,128]{2,1,0:T(8,128)} %get-tuple-element.314, s32[]{:T(128)} %get-tuple-element.313, f32[16,512,128]{2,1,0:T(8,128)} %gather_fusion.2, pred[16]{0:T(512)(128)(4,1)S(1)} %compare_and_fusion.7, f32[512,16,512]{2,0,1:T(8,128)} %fusion.112, f32[16,512]{1,0:T(8,128)S(1)} %multiply_reduce_fusion.5, ...), kind=kOutput, calls=%fused_computation.25.clone.1 | convolution fusion | flops 6464471040 | bytes 21269008 | tf_op jit(solution)/shard_map/cond/branch_0_fun/while/body/eval_jaxpr/tjs,jsw->tw/dot_general | solution.py:14
  537.0 0.6 dynamic_slice.65
  539.5 1.3 constant_dynamic-slice_fusion.9
  540.9 4.1 gather_fusion.3
  545.0 16.2 %fusion.112 = f32[512,16,512]{2,0,1:T(8,128)} fusion(f32[16,64,512]{2,1,0:T(8,128)S(1)} %gather_fusion.3, pred[16]{0:T(512)(128)(4,1)S(1)} %compare_and_fusion.7, f32[64,1,512]{2,1,0:T(1,128)S(1)} %constant_dynamic-slice_fusion.9, pred[]{:T(512)S(6)} %and.57), kind=kOutput, calls=%fused_computation.22.clone.1 | convolution fusion | flops 3221782528 | bytes 19005456 | tf_op jit(solution)/shard_map/cond/branch_0_fun/while/body/eval_jaxpr/dt,jds->tjs/dot_general | solution.py:9
  561.2 0.4 multiply_reduce_fusion.5
  561.5 8.5 %gather_fusion.2 = f32[16,512,128]{2,1,0:T(8,128)} fusion(f32[64,512,128]{2,1,0:T(8,128)} %get-tuple-element.330, s32[1024]{0:T(1024)S(1)} %pad_clamp_fusion.7), kind=kCustom, calls=%fused_computation.1.clone.1 | custom fusion | bytes 8388672 | tf_op jit(solution)/shard_map/cond/branch_0_fun/while/body/eval_jaxpr/jit(_take)/gather | solution.py:71
  570.1 21.5 %fusion.114 = f32[4,512,128]{2,1,0:T(8,128)} fusion(f32[4,512,128]{2,1,0:T(8,128)} %get-tuple-element.314, s32[]{:T(128)} %get-tuple-element.313, f32[16,512,128]{2,1,0:T(8,128)} %gather_fusion.2, pred[16]{0:T(512)(128)(4,1)S(1)} %compare_and_fusion.7, f32[512,16,512]{2,0,1:T(8,128)} %fusion.112, f32[16,512]{1,0:T(8,128)S(1)} %multiply_reduce_fusion.5, ...), kind=kOutput, calls=%fused_computation.25.clone.1 | convolution fusion | flops 6464471040 | bytes 21269008 | tf_op jit(solution)/shard_map/cond/branch_0_fun/while/body/eval_jaxpr/tjs,jsw->tw/dot_general | solution.py:14
  591.6 0.6 dynamic_slice.65
  594.1 1.3 constant_dynamic-slice_fusion.9
  595.4 4.1 gather_fusion.3
  599.5 16.2 %fusion.112 = f32[512,16,512]{2,0,1:T(8,128)} fusion(f32[16,64,512]{2,1,0:T(8,128)S(1)} %gather_fusion.3, pred[16]{0:T(512)(128)(4,1)S(1)} %compare_and_fusion.7, f32[64,1,512]{2,1,0:T(1,128)S(1)} %constant_dynamic-slice_fusion.9, pred[]{:T(512)S(6)} %and.57), kind=kOutput, calls=%fused_computation.22.clone.1 | convolution fusion | flops 3221782528 | bytes 19005456 | tf_op jit(solution)/shard_map/cond/branch_0_fun/while/body/eval_jaxpr/dt,jds->tjs/dot_general | solution.py:9
  615.7 0.4 multiply_reduce_fusion.5
  616.1 8.5 %gather_fusion.2 = f32[16,512,128]{2,1,0:T(8,128)} fusion(f32[64,512,128]{2,1,0:T(8,128)} %get-tuple-element.330, s32[1024]{0:T(1024)S(1)} %pad_clamp_fusion.7), kind=kCustom, calls=%fused_computation.1.clone.1 | custom fusion | bytes 8388672 | tf_op jit(solution)/shard_map/cond/branch_0_fun/while/body/eval_jaxpr/jit(_take)/gather | solution.py:71
  624.6 21.5 %fusion.114 = f32[4,512,128]{2,1,0:T(8,128)} fusion(f32[4,512,128]{2,1,0:T(8,128)} %get-tuple-element.314, s32[]{:T(128)} %get-tuple-element.313, f32[16,512,128]{2,1,0:T(8,128)} %gather_fusion.2, pred[16]{0:T(512)(128)(4,1)S(1)} %compare_and_fusion.7, f32[512,16,512]{2,0,1:T(8,128)} %fusion.112, f32[16,512]{1,0:T(8,128)S(1)} %multiply_reduce_fusion.5, ...), kind=kOutput, calls=%fused_computation.25.clone.1 | convolution fusion | flops 6464471040 | bytes 21269008 | tf_op jit(solution)/shard_map/cond/branch_0_fun/while/body/eval_jaxpr/tjs,jsw->tw/dot_general | solution.py:14
  646.2 0.6 dynamic_slice.65
  648.6 1.3 constant_dynamic-slice_fusion.9
  650.0 4.1 gather_fusion.3
  654.1 16.2 %fusion.112 = f32[512,16,512]{2,0,1:T(8,128)} fusion(f32[16,64,512]{2,1,0:T(8,128)S(1)} %gather_fusion.3, pred[16]{0:T(512)(128)(4,1)S(1)} %compare_and_fusion.7, f32[64,1,512]{2,1,0:T(1,128)S(1)} %constant_dynamic-slice_fusion.9, pred[]{:T(512)S(6)} %and.57), kind=kOutput, calls=%fused_computation.22.clone.1 | convolution fusion | flops 3221782528 | bytes 19005456 | tf_op jit(solution)/shard_map/cond/branch_0_fun/while/body/eval_jaxpr/dt,jds->tjs/dot_general | solution.py:9
  670.3 0.4 multiply_reduce_fusion.5
  670.7 8.5 %gather_fusion.2 = f32[16,512,128]{2,1,0:T(8,128)} fusion(f32[64,512,128]{2,1,0:T(8,128)} %get-tuple-element.330, s32[1024]{0:T(1024)S(1)} %pad_clamp_fusion.7), kind=kCustom, calls=%fused_computation.1.clone.1 | custom fusion | bytes 8388672 | tf_op jit(solution)/shard_map/cond/branch_0_fun/while/body/eval_jaxpr/jit(_take)/gather | solution.py:71
  679.2 21.5 %fusion.114 = f32[4,512,128]{2,1,0:T(8,128)} fusion(f32[4,512,128]{2,1,0:T(8,128)} %get-tuple-element.314, s32[]{:T(128)} %get-tuple-element.313, f32[16,512,128]{2,1,0:T(8,128)} %gather_fusion.2, pred[16]{0:T(512)(128)(4,1)S(1)} %compare_and_fusion.7, f32[512,16,512]{2,0,1:T(8,128)} %fusion.112, f32[16,512]{1,0:T(8,128)S(1)} %multiply_reduce_fusion.5, ...), kind=kOutput, calls=%fused_computation.25.clone.1 | convolution fusion | flops 6464471040 | bytes 21269008 | tf_op jit(solution)/shard_map/cond/branch_0_fun/while/body/eval_jaxpr/tjs,jsw->tw/dot_general | solution.py:14
  700.7 2.0 broadcast.190
  702.7 2.3 constant_dynamic-update-slice_fusion
  705.0 0.0 all-reduce.4.cloned.1.call-update
  705.0 104.8 %all-reduce.4.cloned.1.call-done = f32[6144,128]{1,0:T(8,128)} async-done(((f32[6144,128]{1,0:T(8,128)}), f32[6144,128]{1,0:T(8,128)}) %all-reduce.4.cloned.1.call-update) | async-done | bytes 3145744 | tf_op jit(solution)/shard_map/psum | solution.py:92
  809.8 3.8 copy.95
  (35 shorter events, 0.3 us)
Async XLA Ops:
  6.5 37.7 %copy-start = (f32[6144,128]{1,0:T(8,128)S(1)}, f32[6144,128]{1,0:T(8,128)}, u32[]{:S(2)}) copy-start(f32[6144,128]{1,0:T(8,128)} %param.16) | copy-start | bytes 9437188
  8.1 16.4 %all-to-all-start = ((s32[32,1,2]{2,1,0:T(1,128)}), s32[32,1,2]{2,1,0:T(1,128)S(1)}, u32[]{:S(2)}, u32[]{:S(2)}) async-start(s32[32,1,2]{2,1,0:T(1,128)} %copy.36), calls=%async_computation | async-start | bytes 32768 | tf_op jit(solution)/shard_map/all_to_all | solution.py:33
  39.1 105.0 %all-to-all-start.1 = ((f32[32,2,64,512]{3,2,1,0:T(8,128)}), f32[32,2,64,512]{3,2,1,0:T(8,128)}, u32[]{:S(2)}, u32[]{:S(2)}) async-start(f32[32,2,64,512]{3,2,1,0:T(8,128)} %broadcast_select_fusion.1), calls=%async_computation.1 | async-start | bytes 16777216 | tf_op jit(solution)/shard_map/all_to_all | solution.py:36
  144.0 337.7 %all-to-all-start.2 = ((f32[32,2,512,128]{3,2,1,0:T(8,128)}), f32[32,2,512,128]{3,2,1,0:T(8,128)}, u32[]{:S(2)}, u32[]{:S(2)}) async-start(f32[32,2,512,128]{3,2,1,0:T(8,128)} %broadcast_select_fusion), calls=%async_computation.2 | async-start | bytes 33554432 | tf_op jit(solution)/shard_map/all_to_all | solution.py:37
  155.3 3.3 copy-start.4
  155.3 326.4 %all-reduce.6.cloned.1.call-start = ((), (), s32[]{:S(2)}) async-start(), calls=%async_computation.4 | async-start | bytes 12582912 | tf_op jit(solution)/shard_map/psum | solution.py:59
  167.2 2.3 copy-start.2
  169.4 312.3 %copy-start.3 = (s32[12,8]{0,1:T(8,128)S(1)}, s32[12,8]{0,1:T(8,128)}, u32[]{:S(2)}) copy-start(s32[12,8]{0,1:T(8,128)} %param.20) | copy-start | bytes 1156
  169.5 640.3 %all-reduce.4.cloned.1.call-start = ((), (), s32[]{:S(2)}) async-start(), calls=%async_computation.3 | async-start | bytes 6291456 | tf_op jit(solution)/shard_map/psum | solution.py:92
  705.0 108.6 %copy-start.1 = (f32[6144,128]{1,0:T(8,128)S(1)}, f32[6144,128]{1,0:T(8,128)}, u32[]{:S(2)}) copy-start(f32[6144,128]{1,0:T(8,128)} %param.16) | copy-start | bytes 9437188
Sparse Core Ops, SparseCore 0:
  169.6 312.1 all-reduce.5
  705.1 104.6 all-reduce.3
where the time goes:
time: 823 us; the launch traced here: 820 us
  waiting for transfers between devices  500 us (61%)
  matrix products  154 us (19%)
  local copies, waits for them, and re-layouts  96.2 us (12%)
  starting transfers between devices  26 us (3%)
  other arithmetic  22.5 us (3%)
  between operations  13.5 us (2%)
    psum x1, waiting for transfers between devices, on_device(): lax.psum((table_coords, table_weights), ('grp', 'dev'))  310 us
    psum x1, waiting for transfers between devices, on_device(): total = lax.psum(contribution, 'grp')  105 us
    dot_general x4, matrix products, kernel_sum(): return jnp.einsum('tjs,jsw->tw', kernel, values, precision=high)  86.1 us
    all_to_all x1, waiting for transfers between devices, on_device(): lax.all_to_all(coords, 'dev', split_axis=0, concat_axis=0, tiled=True)  80.8 us
    dot_general x4, matrix products, kernel_sum(): inner = jnp.einsum('dt,jds->tjs', target, sources, precision=high)  64.7 us
    gather x4, local copies, waits for them, and re-layouts, near_leaf(): jnp.take(flat_values, leaf_slots, axis=0)  34 us
  transfers between devices with their start and end apart: 5, of which 4 were waited for; matrix products, arithmetic and copies ran while one was open for 5% of the time, Pallas kernels for 0%

commit v1 on v0

--- a/solution.py
+++ b/solution.py
@@ -89,7 +89,10 @@
         return lax.map(far_leaf, (jnp.arange(targets, dtype=jnp.int32), far_list))
 
     contribution = lax.cond(far_side, far_work, near_work)
-    total = lax.psum(contribution, "grp")
+    proceed_slabs_all = lambda device_axis, a0: lax.all_gather(a0, axis_name=device_axis).sum(
+        axis=0
+    )
+    total = proceed_slabs_all("grp", contribution)
     return total.reshape(column_points, columns)
 
 

time: 823 us -> 870 us (1.057)
  waiting for transfers between devices: 500 us -> 543 us
    all_gather x0 -> x1, waiting for transfers between devices: none -> 148 us  [on_device(): lax.all_gather(a0, axis_name=device_axis).sum(axis=0)]
    psum x1 -> x0, waiting for transfers between devices: 105 us -> none  [on_device(): total = lax.psum(contribution, 'grp')]
  transfers between devices with their start and end apart: 5 -> 5, of which waited for: 4 -> 4; matrix products, arithmetic and copies ran while one was open for 5% -> 4% of each run, Pallas kernels for 0% -> 0%
where the time goes in v1:
time: 870 us; the launch traced here: 867 us
  waiting for transfers between devices  543 us (62%)
  matrix products  154 us (18%)
  local copies, waits for them, and re-layouts  92.5 us (11%)
  other arithmetic  30.1 us (3%)
  starting transfers between devices  26 us (3%)
  between operations  13.5 us (2%)
    psum x1, waiting for transfers between devices, on_device(): lax.psum((table_coords, table_weights), ('grp', 'dev'))  310 us
    all_gather x1, waiting for transfers between devices, on_device(): lax.all_gather(a0, axis_name=device_axis).sum(axis=0)  148 us
    dot_general x4, matrix products, kernel_sum(): return jnp.einsum('tjs,jsw->tw', kernel, values, precision=high)  86.1 us
    all_to_all x1, waiting for transfers between devices, on_device(): lax.all_to_all(coords, 'dev', split_axis=0, concat_axis=0, tiled=True)  80.8 us
    dot_general x4, matrix products, kernel_sum(): inner = jnp.einsum('dt,jds->tjs', target, sources, precision=high)  64.7 us
    gather x4, local copies, waits for them, and re-layouts, near_leaf(): jnp.take(flat_values, leaf_slots, axis=0)  34 us
  transfers between devices with their start and end apart: 5, of which 4 were waited for; matrix products, arithmetic and copies ran while one was open for 4% of the time, Pallas kernels for 0%

profile of v1, /device:TPU:1, one launch (start us, length us, event | category | flops | bytes accessed | tf_op | source)
XLA Modules:
  0.0 867.0 jit_solution(5999367234654284259)
XLA Ops:
  6.5 0.8 fusion.82
  7.4 0.7 copy.36
  8.1 9.4 %all-to-all-start = ((s32[32,1,2]{2,1,0:T(1,128)}), s32[32,1,2]{2,1,0:T(1,128)S(1)}, u32[]{:S(2)}, u32[]{:S(2)}) async-start(s32[32,1,2]{2,1,0:T(1,128)} %copy.36), calls=%async_computation | async-start | bytes 32768 | tf_op jit(solution)/shard_map/all_to_all | solution.py:33
  17.5 2.7 copy.64
  20.2 4.2 all-to-all-done
  24.4 0.1 copy.37
  24.5 0.1 copy.40
  24.6 0.1 reshape.285
  24.7 0.1 copy.38
  24.8 5.7 gather_fusion.4
  30.6 8.5 broadcast_select_fusion.1
  39.1 5.2 all-to-all-start.1
  44.3 7.4 gather_fusion.5
  51.6 11.6 %broadcast_select_fusion = f32[32,2,512,128]{3,2,1,0:T(8,128)} fusion(f32[32,2,512,128]{3,2,1,0:T(8,128)} %bitcast.102, pred[32,2]{1,0:T(8,128)(4,1)S(1)} %copy.38), kind=kLoop, calls=%fused_computation.86 | loop fusion | flops 4194304 | bytes 33554496 | tf_op jit(solution)/shard_map/jit(_take)/select_n | solution.py:35
  63.2 80.8 %all-to-all-done.1 = f32[32,2,64,512]{3,2,1,0:T(8,128)} async-done(((f32[32,2,64,512]{3,2,1,0:T(8,128)}), f32[32,2,64,512]{3,2,1,0:T(8,128)}, u32[]{:S(2)}, u32[]{:S(2)}) %all-to-all-start.1) | async-done | bytes 8388640 | tf_op jit(solution)/shard_map/all_to_all | solution.py:36
  144.0 11.3 %all-to-all-start.2 = ((f32[32,2,512,128]{3,2,1,0:T(8,128)}), f32[32,2,512,128]{3,2,1,0:T(8,128)}, u32[]{:S(2)}, u32[]{:S(2)}) async-start(f32[32,2,512,128]{3,2,1,0:T(8,128)} %broadcast_select_fusion), calls=%async_computation.2 | async-start | bytes 33554432 | tf_op jit(solution)/shard_map/all_to_all | solution.py:37
  155.3 0.0 all-reduce.3.cloned.1.call-start
  155.4 3.3 copy.43
  158.6 2.6 gather_fusion.6
  161.3 0.1 copy.44
  161.3 2.4 broadcast_in_dim.110
  163.8 3.5 fusion.75
  167.2 1.6 broadcast_in_dim.107
  168.8 0.6 fusion.80
  169.4 0.0 all-reduce.3.cloned.1.call-update
  169.5 0.0 all-gather.3.cloned.1.call-start
  169.5 1.9 reshape.193
  171.4 310.3 %all-reduce.3.cloned.1.call-done = (f32[32,64,256]{2,1,0:T(8,128)}, f32[32,256,128]{2,1,0:T(8,128)}) async-done(((f32[32,64,256]{2,1,0:T(8,128)}, f32[32,256,128]{2,1,0:T(8,128)}), (f32[32,64,256]{2,1,0:T(8,128)}, f32[32,256,128]{2,1,0:T(8,128)})) %all-reduce.3.cloned.1.call-update) | async-done | bytes 6291472 | tf_op jit(solution)/shard_map/psum | solution.py:59
  481.8 223.2 %conditional.1 = (f32[12,512,128]{2,1,0:T(8,128)}) conditional(s32[]{:T(128)} %convert_element_type.3, (s32[]{:T(128)}, s32[12,16]{1,0:T(8,128)}, f32[32,2,64,512]{3,2,1,0:T(8,128)}, f32[32,2,512,128]{3,2,1,0:T(8,128)}, f32[64,12,512]{2,1,0:T(8,128)}) %tuple.20, (f32[64,12,512]{2,1,0:T(8,128)}, s32[12,8]{0,1:T(8,128)S(1)}, f32[32,64,256]{2,1,0:T(8,128)}, ...), branch_computations={%region_2.0_spmd, %region_7.13_spmd} | conditional | flops 9687917568 | bytes 60630836 | solution.py:91
  481.8 0.7 constant_dynamic-slice_fusion.2
  482.4 218.3 %while.19 = (s32[]{:T(128)}, f32[4,512,128]{2,1,0:T(8,128)}, s32[4]{0:T(128)S(1)}, f32[64,12,512]{2,1,0:T(8,128)}, s32[4,16]{1,0:T(4,128)S(1)}, /*index=5*/f32[6...) while((s32[]{:T(128)}, f32[4,512,128]{2,1,0:T(8,128)}, ...), condition=%wide.region_6.7_spmd, body=%wide.region_3.6_spmd.sunk | while | flops 9687917568 | bytes 55387260 | solution.py:74
  482.5 0.6 dynamic_slice.65
  484.9 1.3 constant_dynamic-slice_fusion.9
  486.3 4.1 gather_fusion.3
  490.4 16.2 %fusion.112 = f32[512,16,512]{2,0,1:T(8,128)} fusion(f32[16,64,512]{2,1,0:T(8,128)S(1)} %gather_fusion.3, pred[16]{0:T(512)(128)(4,1)S(1)} %compare_and_fusion.7, f32[64,1,512]{2,1,0:T(1,128)S(1)} %constant_dynamic-slice_fusion.9, pred[]{:T(512)S(6)} %and.57), kind=kOutput, calls=%fused_computation.22.clone.1 | convolution fusion | flops 3221782528 | bytes 19005456 | tf_op jit(solution)/shard_map/cond/branch_0_fun/while/body/eval_jaxpr/dt,jds->tjs/dot_general | solution.py:9
  506.6 0.4 multiply_reduce_fusion.5
  507.0 8.5 gather_fusion.2
  515.5 21.5 %fusion.114 = f32[4,512,128]{2,1,0:T(8,128)} fusion(f32[4,512,128]{2,1,0:T(8,128)} %get-tuple-element.314, s32[]{:T(128)} %get-tuple-element.313, f32[16,512,128]{2,1,0:T(8,128)} %gather_fusion.2, pred[16]{0:T(512)(128)(4,1)S(1)} %compare_and_fusion.7, f32[512,16,512]{2,0,1:T(8,128)} %fusion.112, f32[16,512]{1,0:T(8,128)S(1)} %multiply_reduce_fusion.5, ...), kind=kOutput, calls=%fused_computation.25.clone.1 | convolution fusion | flops 6464471040 | bytes 21269008 | tf_op jit(solution)/shard_map/cond/branch_0_fun/while/body/eval_jaxpr/tjs,jsw->tw/dot_general | solution.py:14
  537.0 0.6 dynamic_slice.65
  539.5 1.3 constant_dynamic-slice_fusion.9
  540.9 4.1 gather_fusion.3
  545.0 16.2 %fusion.112 = f32[512,16,512]{2,0,1:T(8,128)} fusion(f32[16,64,512]{2,1,0:T(8,128)S(1)} %gather_fusion.3, pred[16]{0:T(512)(128)(4,1)S(1)} %compare_and_fusion.7, f32[64,1,512]{2,1,0:T(1,128)S(1)} %constant_dynamic-slice_fusion.9, pred[]{:T(512)S(6)} %and.57), kind=kOutput, calls=%fused_computation.22.clone.1 | convolution fusion | flops 3221782528 | bytes 19005456 | tf_op jit(solution)/shard_map/cond/branch_0_fun/while/body/eval_jaxpr/dt,jds->tjs/dot_general | solution.py:9
  561.2 0.4 multiply_reduce_fusion.5
  561.5 8.5 gather_fusion.2
  570.1 21.5 %fusion.114 = f32[4,512,128]{2,1,0:T(8,128)} fusion(f32[4,512,128]{2,1,0:T(8,128)} %get-tuple-element.314, s32[]{:T(128)} %get-tuple-element.313, f32[16,512,128]{2,1,0:T(8,128)} %gather_fusion.2, pred[16]{0:T(512)(128)(4,1)S(1)} %compare_and_fusion.7, f32[512,16,512]{2,0,1:T(8,128)} %fusion.112, f32[16,512]{1,0:T(8,128)S(1)} %multiply_reduce_fusion.5, ...), kind=kOutput, calls=%fused_computation.25.clone.1 | convolution fusion | flops 6464471040 | bytes 21269008 | tf_op jit(solution)/shard_map/cond/branch_0_fun/while/body/eval_jaxpr/tjs,jsw->tw/dot_general | solution.py:14
  591.6 0.6 dynamic_slice.65
  594.1 1.3 constant_dynamic-slice_fusion.9
  595.4 4.1 gather_fusion.3
  599.5 16.2 %fusion.112 = f32[512,16,512]{2,0,1:T(8,128)} fusion(f32[16,64,512]{2,1,0:T(8,128)S(1)} %gather_fusion.3, pred[16]{0:T(512)(128)(4,1)S(1)} %compare_and_fusion.7, f32[64,1,512]{2,1,0:T(1,128)S(1)} %constant_dynamic-slice_fusion.9, pred[]{:T(512)S(6)} %and.57), kind=kOutput, calls=%fused_computation.22.clone.1 | convolution fusion | flops 3221782528 | bytes 19005456 | tf_op jit(solution)/shard_map/cond/branch_0_fun/while/body/eval_jaxpr/dt,jds->tjs/dot_general | solution.py:9
  615.7 0.4 multiply_reduce_fusion.5
  616.1 8.5 gather_fusion.2
  624.6 21.5 %fusion.114 = f32[4,512,128]{2,1,0:T(8,128)} fusion(f32[4,512,128]{2,1,0:T(8,128)} %get-tuple-element.314, s32[]{:T(128)} %get-tuple-element.313, f32[16,512,128]{2,1,0:T(8,128)} %gather_fusion.2, pred[16]{0:T(512)(128)(4,1)S(1)} %compare_and_fusion.7, f32[512,16,512]{2,0,1:T(8,128)} %fusion.112, f32[16,512]{1,0:T(8,128)S(1)} %multiply_reduce_fusion.5, ...), kind=kOutput, calls=%fused_computation.25.clone.1 | convolution fusion | flops 6464471040 | bytes 21269008 | tf_op jit(solution)/shard_map/cond/branch_0_fun/while/body/eval_jaxpr/tjs,jsw->tw/dot_general | solution.py:14
  646.2 0.6 dynamic_slice.65
  648.6 1.3 constant_dynamic-slice_fusion.9
  650.0 4.1 gather_fusion.3
  654.1 16.2 %fusion.112 = f32[512,16,512]{2,0,1:T(8,128)} fusion(f32[16,64,512]{2,1,0:T(8,128)S(1)} %gather_fusion.3, pred[16]{0:T(512)(128)(4,1)S(1)} %compare_and_fusion.7, f32[64,1,512]{2,1,0:T(1,128)S(1)} %constant_dynamic-slice_fusion.9, pred[]{:T(512)S(6)} %and.57), kind=kOutput, calls=%fused_computation.22.clone.1 | convolution fusion | flops 3221782528 | bytes 19005456 | tf_op jit(solution)/shard_map/cond/branch_0_fun/while/body/eval_jaxpr/dt,jds->tjs/dot_general | solution.py:9
  670.3 0.4 multiply_reduce_fusion.5
  670.7 8.5 gather_fusion.2
  679.2 21.5 %fusion.114 = f32[4,512,128]{2,1,0:T(8,128)} fusion(f32[4,512,128]{2,1,0:T(8,128)} %get-tuple-element.314, s32[]{:T(128)} %get-tuple-element.313, f32[16,512,128]{2,1,0:T(8,128)} %gather_fusion.2, pred[16]{0:T(512)(128)(4,1)S(1)} %compare_and_fusion.7, f32[512,16,512]{2,0,1:T(8,128)} %fusion.112, f32[16,512]{1,0:T(8,128)S(1)} %multiply_reduce_fusion.5, ...), kind=kOutput, calls=%fused_computation.25.clone.1 | convolution fusion | flops 6464471040 | bytes 21269008 | tf_op jit(solution)/shard_map/cond/branch_0_fun/while/body/eval_jaxpr/tjs,jsw->tw/dot_general | solution.py:14
  700.7 2.0 broadcast.190
  702.7 2.3 constant_dynamic-update-slice_fusion
  705.0 0.0 all-gather.3.cloned.1.call-update
  705.0 147.6 %all-gather.3.cloned.1.call-done = f32[48,512,128]{2,1,0:T(8,128)} async-done(((f32[12,512,128]{2,1,0:T(8,128)}), f32[48,512,128]{2,1,0:T(8,128)}) %all-gather.3.cloned.1.call-update) | async-done | bytes 12582928 | tf_op jit(solution)/shard_map/all_gather | solution.py:92
  852.6 7.6 reduce_sum.45
  (35 shorter events, 0.3 us)
Async XLA Ops:
  6.5 37.7 %copy-start = (f32[6144,128]{1,0:T(8,128)S(1)}, f32[6144,128]{1,0:T(8,128)}, u32[]{:S(2)}) copy-start(f32[6144,128]{1,0:T(8,128)} %param.16) | copy-start | bytes 9437188
  8.1 16.4 %all-to-all-start = ((s32[32,1,2]{2,1,0:T(1,128)}), s32[32,1,2]{2,1,0:T(1,128)S(1)}, u32[]{:S(2)}, u32[]{:S(2)}) async-start(s32[32,1,2]{2,1,0:T(1,128)} %copy.36), calls=%async_computation | async-start | bytes 32768 | tf_op jit(solution)/shard_map/all_to_all | solution.py:33
  39.1 105.0 %all-to-all-start.1 = ((f32[32,2,64,512]{3,2,1,0:T(8,128)}), f32[32,2,64,512]{3,2,1,0:T(8,128)}, u32[]{:S(2)}, u32[]{:S(2)}) async-start(f32[32,2,64,512]{3,2,1,0:T(8,128)} %broadcast_select_fusion.1), calls=%async_computation.1 | async-start | bytes 16777216 | tf_op jit(solution)/shard_map/all_to_all | solution.py:36
  144.0 337.7 %all-to-all-start.2 = ((f32[32,2,512,128]{3,2,1,0:T(8,128)}), f32[32,2,512,128]{3,2,1,0:T(8,128)}, u32[]{:S(2)}, u32[]{:S(2)}) async-start(f32[32,2,512,128]{3,2,1,0:T(8,128)} %broadcast_select_fusion), calls=%async_computation.2 | async-start | bytes 33554432 | tf_op jit(solution)/shard_map/all_to_all | solution.py:37
  155.3 3.3 copy-start.4
  155.3 326.4 %all-reduce.3.cloned.1.call-start = ((), (), s32[]{:S(2)}) async-start(), calls=%async_computation.4 | async-start | bytes 12582912 | tf_op jit(solution)/shard_map/psum | solution.py:59
  167.2 2.3 copy-start.2
  169.4 312.3 %copy-start.3 = (s32[12,8]{0,1:T(8,128)S(1)}, s32[12,8]{0,1:T(8,128)}, u32[]{:S(2)}) copy-start(s32[12,8]{0,1:T(8,128)} %param.20) | copy-start | bytes 1156
  169.5 683.1 %all-gather.3.cloned.1.call-start = ((), (), s32[]{:S(2)}) async-start(), calls=%async_computation.3 | async-start | bytes 15728640 | tf_op jit(solution)/shard_map/all_gather | solution.py:92
  852.6 7.6 copy-start.1
Sparse Core Ops, SparseCore 0:
  169.6 312.1 all-reduce.2
  705.1 147.4 all-gather.2
